TPU v7x, 32 devices: a whole 2x2x4 slice. The times are simulated.
32 devices in a mesh: seq: 16 (over z, y, x), chan: 2 (over core).
Axes of the slice: x: 2, y: 2, z: 4, core: 2. Of those that a mesh axis runs over, the one named last changes fastest.
Arguments:
- streams: bfloat16 [3, 512, 4096], P(None, 'chan', 'seq'), may hold values from -6 to 6
- short_filters: float32 [3, 7, 512], P(None, None, 'chan'), may hold values from -2 to 2
- long_filter: float32 [64, 4096], P(None, 'seq'), may hold values from -2 to 2
- skip_gain: float32 [512], P('chan'), may hold values from 0.3 to 1.5
- out_grad: bfloat16 [512, 4096], P('chan', 'seq'), may hold values from -6 to 6
Outputs:
- stream_grad: bfloat16 [3, 512, 4096], P(None, 'chan', 'seq')
- filter_grad: float32 [64, 4096], P(None, 'seq')
All inputs are finite; a program needn't handle non-finite values.
Results may differ from a plain program's by a relative error of at most 0.0004.
Values may be sent and summed in bfloat16 or wider, within the bound.
A program may use at most 64 MiB of HBM per device.

v0:
```python
import math
import jax
import jax.numpy as jnp
from jax import lax
from jax.sharding import PartitionSpec as P


def partner_2(value, axis, apart):
    mask = 2**apart
    pairs = [(source, source ^ mask) for source in range(lax.axis_size(axis))]
    return lax.ppermute(value, axis, pairs)


def shifted(shard, axis, by):
    length = lax.axis_size(axis)
    pairs = [(i, i + by) for i in range(length) if 0 <= i + by < length]
    return lax.ppermute(shard, axis, pairs)


def rotate(real_part, imag_part, cosine, sine_part):
    return (real_part * cosine - imag_part * sine_part, real_part * sine_part + imag_part * cosine)


def split_halves(signal):
    middle = signal.shape[-1] // 2
    return (signal[..., :middle], signal[..., middle:])


def join_halves(real_part, imag_part):
    return jnp.concatenate([real_part, imag_part], axis=-1)


def complex_product(first_op, second_op, conjugate):
    first_re, first_im = split_halves(first_op)
    second_re, second_im = split_halves(second_op)
    if conjugate:
        second_im = -second_im
    return join_halves(
        first_re * second_re - first_im * second_im, first_re * second_im + first_im * second_re
    )


def dft_table(length, direction, scaling):
    indices = jnp.arange(length, dtype=jnp.int32)
    phases = (indices[:, None] * indices[None, :] % length).astype(jnp.float32) * (
        direction * 2.0 * math.pi / length
    )
    cosine = jnp.cos(phases) * scaling
    sine_part = jnp.sin(phases) * scaling
    upper_rows = jnp.concatenate([cosine, sine_part], axis=1)
    lower_rows = jnp.concatenate([-sine_part, cosine], axis=1)
    return jnp.concatenate([upper_rows, lower_rows], axis=0)


def section_count():
    return lax.axis_size("seq").bit_length() - 1


def bit_reverse(position, sections):
    result = jnp.zeros((), jnp.int32)
    for bit_level in range(sections):
        result = result + position // (1 << bit_level) % 2 * (1 << sections - 1 - bit_level)
    return result


def held_index():
    return bit_reverse(lax.axis_index("seq"), section_count())


def inner_twiddle(signal, held, direction):
    length = signal.shape[-1] // 2
    seq_total = length * lax.axis_size("seq")
    indices = jnp.arange(length, dtype=jnp.int32)
    phases = (indices * held % seq_total).astype(jnp.float32) * (
        direction * 2.0 * math.pi / seq_total
    )
    real_part, imag_part = split_halves(signal)
    turned_re, turned_im = rotate(real_part, imag_part, jnp.cos(phases), jnp.sin(phases))
    return join_halves(turned_re, turned_im)


def forward_sections(signal):
    position = lax.axis_index("seq")
    sections = section_count()
    for bit_level in reversed(range(sections)):
        half_span = 1 << bit_level
        partner = partner_2(signal, "seq", bit_level)
        upper_side = position // half_span % 2 == 1
        phases = (position % half_span).astype(jnp.float32) * (-math.pi / half_span)
        diff_re, diff_im = split_halves(partner - signal)
        turned_re, turned_im = rotate(diff_re, diff_im, jnp.cos(phases), jnp.sin(phases))
        signal = jnp.where(upper_side, join_halves(turned_re, turned_im), signal + partner)
    return signal


def inverse_sections(signal):
    position = lax.axis_index("seq")
    sections = section_count()
    for bit_level in range(sections):
        half_span = 1 << bit_level
        partner = partner_2(signal, "seq", bit_level)
        upper_side = position // half_span % 2 == 1
        phases = (position % half_span).astype(jnp.float32) * (math.pi / half_span)
        source = jnp.where(upper_side, signal, partner)
        base_term = jnp.where(upper_side, partner, signal)
        source_re, source_im = split_halves(source)
        turned_re, turned_im = rotate(source_re, source_im, jnp.cos(phases), jnp.sin(phases))
        turned = join_halves(turned_re, turned_im)
        signal = 0.5 * jnp.where(upper_side, base_term - turned, base_term + turned)
    return signal


def forward_dft(signal, dft_matrix):
    signal = forward_sections(signal)
    signal = inner_twiddle(signal, held_index(), -1.0)
    return jnp.dot(
        signal, dft_matrix, precision=lax.Precision.HIGHEST, preferred_element_type=jnp.float32
    )


def inverse_dft(spectra, dft_matrix):
    signal = jnp.dot(
        spectra, dft_matrix, precision=lax.Precision.HIGHEST, preferred_element_type=jnp.float32
    )
    signal = inner_twiddle(signal, held_index(), 1.0)
    return inverse_sections(signal)


def local(streams, short_filters, long_filter, skip_gain, out_grad):
    tap_count = short_filters.shape[1]
    reach_back = tap_count - 1
    channels_dev = streams.shape[1]
    length = streams.shape[2]
    filters = long_filter.shape[0]
    members = channels_dev // filters
    devices = lax.axis_size("seq")
    position = lax.axis_index("seq")
    seq_total = length * devices
    preceding = shifted(streams[:, :, length - reach_back :], "seq", 1)
    extended = jnp.concatenate([preceding, streams], axis=2).astype(jnp.float32)
    filtered = jnp.zeros(streams.shape, jnp.float32)
    for offset in range(tap_count):
        filtered = (
            filtered
            + short_filters[:, offset, :, None]
            * extended[:, :, reach_back - offset : reach_back - offset + length]
        )
    gate_out = filtered[0]
    gate_in = filtered[1]
    values = filtered[2]
    gated_prod = gate_in * values
    out_float = out_grad.astype(jnp.float32)
    gate_grad = out_float * gate_out
    signals = jnp.concatenate([gated_prod, gate_grad, long_filter], axis=0)
    twist_phase = (position * length + jnp.arange(length, dtype=jnp.int32)).astype(jnp.float32) * (
        -math.pi / seq_total
    )
    twist_re = jnp.cos(twist_phase)
    twist_im = jnp.sin(twist_phase)
    even_part = join_halves(signals, jnp.zeros_like(signals))
    odd_part = join_halves(signals * twist_re, signals * twist_im)
    spectra = forward_dft(
        jnp.concatenate([even_part, odd_part], axis=0), dft_table(length, -1.0, 1.0)
    )
    row_count = signals.shape[0]
    halves = (spectra[:row_count], spectra[row_count:])
    filter_specs = (halves[0][2 * channels_dev :], halves[1][2 * channels_dev :])
    products = []
    for half_index in range(2):
        part_spec = halves[half_index]
        gated_spec = part_spec[:channels_dev]
        grad_spec = part_spec[channels_dev : 2 * channels_dev]
        wide_filter = jnp.tile(filter_specs[half_index], (members, 1))
        products.append(complex_product(gated_spec, wide_filter, False))
        products.append(complex_product(grad_spec, wide_filter, True))
        products.append(
            complex_product(grad_spec, gated_spec, True)
            .reshape(members, filters, 2 * length)
            .sum(axis=0)
        )
    time_rows = inverse_dft(jnp.concatenate(products, axis=0), dft_table(length, 1.0, 1.0 / length))
    part_rows = 2 * channels_dev + filters
    even_re, even_im = split_halves(time_rows[:part_rows])
    odd_re, odd_im = split_halves(time_rows[part_rows:])
    combined = 0.5 * (even_re + twist_re * odd_re + twist_im * odd_im)
    conv_part = combined[:channels_dev]
    corr_part = combined[channels_dev : 2 * channels_dev]
    filter_local = combined[2 * channels_dev :]
    conv_out = conv_part + skip_gain[:, None] * gated_prod
    gated_grad = corr_part + skip_gain[:, None] * gate_grad
    members_total = channels_dev * lax.axis_size("chan") // filters
    filter_grad = lax.psum(filter_local, "chan") * (1.0 / math.sqrt(members_total * seq_total))
    grads_in = jnp.stack([out_float * conv_out, gated_grad * values, gated_grad * gate_in])
    following = shifted(grads_in[:, :, :reach_back], "seq", -1)
    extended_grad = jnp.concatenate([grads_in, following], axis=2)
    result = jnp.zeros(grads_in.shape, jnp.float32)
    for offset in range(tap_count):
        result = (
            result
            + short_filters[:, offset, :, None] * extended_grad[:, :, offset : offset + length]
        )
    return (result.astype(jnp.bfloat16), filter_grad)


def solution(mesh):
    in_specs = (
        P(None, "chan", "seq"),
        P(None, None, "chan"),
        P(None, "seq"),
        P("chan"),
        P("chan", "seq"),
    )
    out_specs = (P(None, "chan", "seq"), P(None, "seq"))
    return jax.shard_map(local, mesh=mesh, in_specs=in_specs, out_specs=out_specs, check_vma=False)
```

profile of v0, /device:TPU:0, one launch (start us, length us, event | category | flops | bytes accessed | tf_op | source)
XLA Modules:
  0.0 611.4 jit_solution(11527315104026521100)
XLA Ops:
  7.2 1.2 copy.14
  8.4 4.8 collective-permute-start
  13.2 1.0 fusion.52
  14.4 1.0 copy.13
  15.4 1.0 copy.16
  16.5 0.6 fusion.26
  17.5 1.9 select_maximum_fusion
  19.4 3.4 collective-permute-start.1
  23.0 100.9 %collective-permute-done.1 = f32[1152,512]{0,1:T(8,128)} collective-permute-done((f32[1152,512]{0,1:T(8,128)}, f32[1152,512]{0,1:T(8,128)}, u32[]{:S(2)}, u32[]{:S(2)}) %collective-permute-start.1) | collective-permute-done | bytes 2359328 | tf_op jit(solution)/shard_map/ppermute | solution.py:11
  123.9 2.1 fusion.50
  126.3 2.5 maximum_select_fusion
  128.8 0.7 collective-permute-start.2
  129.7 51.3 %collective-permute-done.2 = f32[1152,512]{0,1:T(8,128)} collective-permute-done((f32[1152,512]{0,1:T(8,128)S(1)}, f32[1152,512]{0,1:T(8,128)}, u32[]{:S(2)}, u32[]{:S(2)}) %collective-permute-start.2) | collective-permute-done | bytes 2359328 | tf_op jit(solution)/shard_map/ppermute | solution.py:11
  181.0 1.9 sub.100
  183.2 3.5 maximum_select_fusion.1
  186.7 1.5 collective-permute-start.3
  188.4 50.0 %collective-permute-done.3 = f32[1152,512]{0,1:T(8,128)S(1)} collective-permute-done((f32[1152,512]{0,1:T(8,128)}, f32[1152,512]{0,1:T(8,128)S(1)}, u32[]{:S(2)}, u32[]{:S(2)}) %collective-permute-start.3) | collective-permute-done | bytes 2359328 | tf_op jit(solution)/shard_map/ppermute | solution.py:11
  238.4 2.8 sub.102
  241.4 2.8 maximum_select_fusion.2
  244.2 1.6 collective-permute-start.4
  245.8 0.7 multiply_sine_fusion.1
  246.5 1.0 fusion.42
  247.5 1.7 fusion.43
  249.2 1.0 multiply_sine_fusion
  250.2 1.8 sine_multiply_fusion
  252.0 42.9 %collective-permute-done.4 = f32[1152,512]{0,1:T(8,128)} collective-permute-done((f32[1152,512]{0,1:T(8,128)S(1)}, f32[1152,512]{0,1:T(8,128)}, u32[]{:S(2)}, u32[]{:S(2)}) %collective-permute-start.4) | collective-permute-done | bytes 2359328 | tf_op jit(solution)/shard_map/ppermute | solution.py:11
  295.0 1.9 sub.104
  297.0 2.1 maximum_select_fusion.3
  299.1 0.3 multiply_subtract_fusion.5
  299.5 4.0 fusion
  303.5 0.9 multiply_subtract_fusion.10
  304.5 1.0 multiply_subtract_fusion.11
  305.6 0.7 reduce_sum.19
  306.3 1.1 pad_maximum_fusion.8
  307.4 0.7 reduce_sum.18
  308.5 0.5 copy-done.16
  309.7 4.8 fusion.11
  314.5 0.3 multiply_subtract_fusion.4
  315.0 1.6 collective-permute-start.5
  316.6 48.1 %collective-permute-done.5 = f32[1152,512]{0,1:T(8,128)S(1)} collective-permute-done((f32[1152,512]{0,1:T(8,128)S(1)}, f32[1152,512]{0,1:T(8,128)S(1)}, u32[]{:S(2)}, u32[]{:S(2)}) %collective-permute-start.5) | collective-permute-done | bytes 2359328 | tf_op jit(solution)/shard_map/ppermute | solution.py:11
  365.1 0.6 select_multiply_fusion.3
  365.8 1.6 collective-permute-start.6
  367.5 47.1 %collective-permute-done.6 = f32[1152,512]{0,1:T(8,128)} collective-permute-done((f32[1152,512]{0,1:T(8,128)S(1)}, f32[1152,512]{0,1:T(8,128)}, u32[]{:S(2)}, u32[]{:S(2)}) %collective-permute-start.6) | collective-permute-done | bytes 2359328 | tf_op jit(solution)/shard_map/ppermute | solution.py:11
  414.6 1.9 broadcast_select_fusion.1
  416.8 1.8 select_multiply_fusion.2
  418.6 5.1 collective-permute-start.7
  423.9 46.9 %collective-permute-done.7 = f32[1152,512]{0,1:T(8,128)S(1)} collective-permute-done((f32[1152,512]{0,1:T(8,128)}, f32[1152,512]{0,1:T(8,128)S(1)}, u32[]{:S(2)}, u32[]{:S(2)}) %collective-permute-start.7) | collective-permute-done | bytes 2359328 | tf_op jit(solution)/shard_map/ppermute | solution.py:11
  471.1 1.2 copy-done.3
  472.6 2.1 select_multiply_fusion.1
  474.6 5.0 collective-permute-start.8
  479.8 96.8 %collective-permute-done.8 = f32[1152,512]{0,1:T(8,128)} collective-permute-done((f32[1152,512]{0,1:T(8,128)S(1)}, f32[1152,512]{0,1:T(8,128)}, u32[]{:S(2)}, u32[]{:S(2)}) %collective-permute-start.8) | collective-permute-done | bytes 2359328 | tf_op jit(solution)/shard_map/ppermute | solution.py:11
  576.6 1.9 broadcast_select_fusion.3
  578.8 0.4 select_multiply_fusion
  579.2 0.3 copy-done.24
  579.5 0.5 fusion.33
  580.0 0.6 copy-done.5
  580.8 1.3 collective-permute-start.9
  582.1 0.7 slice.361
  582.8 3.7 collective-permute-done.9
  586.6 0.7 fusion.20
  587.3 0.9 copy.17
  588.2 14.7 %all-reduce.3.cloned.1.call-done = f32[64,256]{0,1:T(8,128)} async-done(((f32[64,256]{0,1:T(8,128)}), f32[64,256]{0,1:T(8,128)}) %all-reduce.3.cloned.1.call-update) | async-done | bytes 65552 | tf_op jit(solution)/shard_map/psum | solution.py:192
  602.9 0.9 broadcast_multiply_fusion.2
  603.9 0.7 copy.18
  (95 shorter events, 4.3 us)
Async XLA Ops:
  7.2 595.8 %all-reduce.3.cloned.1.call-start = ((), (), s32[]{:S(2)}) async-start(), calls=%async_computation | async-start | bytes 262144 | tf_op jit(solution)/shard_map/psum | solution.py:192
  8.4 8.0 %collective-permute-start = (bf16[3,256,6]{1,2,0:T(8,128)(2,1)S(1)}, bf16[3,256,6]{1,2,0:T(8,128)(2,1)S(1)}, u32[]{:S(2)}, u32[]{:S(2)}) collective-permute-start(bf16[3,256,6]{1,2,0:T(8,128)(2,1)S(1)} %slice.304), channel_id=1, source_target_pairs={{0,2},{2,4},{4,6},{6,8},{8,10},{10,12},{12,14},{14,16},{16,18},{18... | collective-permute-start | bytes 27656 | tf_op jit(solution)/shard_map/ppermute | solution.py:17
  14.3 2.9 copy-start.17
  14.3 2.9 copy-start.19
  14.4 2.9 copy-start.23
  14.4 2.9 copy-start.25
  14.4 2.8 copy-start.21
  15.4 1.8 copy-start.6
  17.2 2.2 copy-start.4
  17.5 108.5 %copy-start = (f32[576,256]{0,1:T(8,128)}, f32[576,256]{0,1:T(8,128)S(1)}, u32[]{:S(2)}) copy-start(f32[576,256]{0,1:T(8,128)S(1)} %get-tuple-element.46) | copy-start | bytes 1769476
  17.5 108.5 %copy-start.1 = (f32[576,256]{0,1:T(8,128)}, f32[576,256]{0,1:T(8,128)S(1)}, u32[]{:S(2)}) copy-start(f32[576,256]{0,1:T(8,128)S(1)} %get-tuple-element.47) | copy-start | bytes 1769476
  19.4 104.5 %collective-permute-start.1 = (f32[1152,512]{0,1:T(8,128)}, f32[1152,512]{0,1:T(8,128)}, u32[]{:S(2)}, u32[]{:S(2)}) collective-permute-start(f32[1152,512]{0,1:T(8,128)} %select_maximum_fusion), channel_id=1, source_target_pairs={{0,16},{2,18},{4,20},{6,22},{8,24},{10,26},{12,28},{14,30},{16,0},... | collective-permute-start | bytes 7077896 | tf_op jit(solution)/shard_map/ppermute | solution.py:11
  128.8 52.3 %collective-permute-start.2 = (f32[1152,512]{0,1:T(8,128)S(1)}, f32[1152,512]{0,1:T(8,128)}, u32[]{:S(2)}, u32[]{:S(2)}) collective-permute-start(f32[1152,512]{0,1:T(8,128)S(1)} %maximum_select_fusion), channel_id=1, source_target_pairs={{0,8},{2,10},{4,12},{6,14},{8,0},{10,2},{12,4},{14,6},{16,24},{18,... | collective-permute-start | bytes 7077896 | tf_op jit(solution)/shard_map/ppermute | solution.py:11
  186.7 51.7 %collective-permute-start.3 = (f32[1152,512]{0,1:T(8,128)}, f32[1152,512]{0,1:T(8,128)S(1)}, u32[]{:S(2)}, u32[]{:S(2)}) collective-permute-start(f32[1152,512]{0,1:T(8,128)} %maximum_select_fusion.1), channel_id=1, source_target_pairs={{0,4},{2,6},{4,0},{6,2},{8,12},{10,14},{12,8},{14,10},{16,20},{18,... | collective-permute-start | bytes 7077896 | tf_op jit(solution)/shard_map/ppermute | solution.py:11
  238.4 2.8 copy-start.2
  244.2 50.7 %collective-permute-start.4 = (f32[1152,512]{0,1:T(8,128)S(1)}, f32[1152,512]{0,1:T(8,128)}, u32[]{:S(2)}, u32[]{:S(2)}) collective-permute-start(f32[1152,512]{0,1:T(8,128)S(1)} %maximum_select_fusion.2), channel_id=1, source_target_pairs={{0,2},{2,0},{4,6},{6,4},{8,10},{10,8},{12,14},{14,12},{16,18},{18,... | collective-permute-start | bytes 7077896 | tf_op jit(solution)/shard_map/ppermute | solution.py:11
  308.1 0.9 copy-start.16
  308.1 1.0 copy-start.10
  308.2 1.1 copy-start.11
  308.3 1.0 copy-start.8
  308.3 1.1 copy-start.9
  308.3 1.2 copy-start.15
  308.3 1.2 copy-start.12
  308.3 1.3 copy-start.13
  308.3 1.4 copy-start.14
  309.7 4.8 copy-start.27
  309.7 4.8 copy-start.28
  315.0 49.7 %collective-permute-start.5 = (f32[1152,512]{0,1:T(8,128)S(1)}, f32[1152,512]{0,1:T(8,128)S(1)}, u32[]{:S(2)}, u32[]{:S(2)}) collective-permute-start(f32[1152,512]{0,1:T(8,128)S(1)} %pad_maximum_fusion), channel_id=1, source_target_pairs={{0,2},{2,0},{4,6},{6,4},{8,10},{10,8},{12,14},{14,12},{16,18},{18,... | collective-permute-start | bytes 7077896 | tf_op jit(solution)/shard_map/ppermute | solution.py:11
  365.8 48.9 %collective-permute-start.6 = (f32[1152,512]{0,1:T(8,128)S(1)}, f32[1152,512]{0,1:T(8,128)}, u32[]{:S(2)}, u32[]{:S(2)}) collective-permute-start(f32[1152,512]{0,1:T(8,128)S(1)} %select_multiply_fusion.3), channel_id=1, source_target_pairs={{0,4},{2,6},{4,0},{6,2},{8,12},{10,14},{12,8},{14,10},{16,20},{18,... | collective-permute-start | bytes 7077896 | tf_op jit(solution)/shard_map/ppermute | solution.py:11
  418.6 52.2 %collective-permute-start.7 = (f32[1152,512]{0,1:T(8,128)}, f32[1152,512]{0,1:T(8,128)S(1)}, u32[]{:S(2)}, u32[]{:S(2)}) collective-permute-start(f32[1152,512]{0,1:T(8,128)} %select_multiply_fusion.2), channel_id=1, source_target_pairs={{0,8},{2,10},{4,12},{6,14},{8,0},{10,2},{12,4},{14,6},{16,24},{18,... | collective-permute-start | bytes 7077896 | tf_op jit(solution)/shard_map/ppermute | solution.py:11
  470.8 1.5 copy-start.3
  474.6 102.0 %collective-permute-start.8 = (f32[1152,512]{0,1:T(8,128)S(1)}, f32[1152,512]{0,1:T(8,128)}, u32[]{:S(2)}, u32[]{:S(2)}) collective-permute-start(f32[1152,512]{0,1:T(8,128)S(1)} %select_multiply_fusion.1), channel_id=1, source_target_pairs={{0,16},{2,18},{4,20},{6,22},{8,24},{10,26},{12,28},{14,30},{16,0},... | collective-permute-start | bytes 7077896 | tf_op jit(solution)/shard_map/ppermute | solution.py:11
  578.8 0.7 copy-start.24
  578.8 0.7 copy-start.26
  579.5 1.1 copy-start.5
  579.5 1.1 copy-start.7
  579.5 1.1 copy-start.29
  580.7 5.9 copy-start.18
  580.7 5.9 copy-start.20
  580.7 5.9 copy-start.22
  580.8 5.7 collective-permute-start.9
Sparse Core Ops, SparseCore 0:
  582.9 19.9 all-reduce.2
where the time goes:
time: 612 us; the launch traced here: 611 us
  waiting for transfers between devices  503 us (82%)
  other arithmetic  47.7 us (8%)
  starting transfers between devices  26.7 us (4%)
  between operations  15.8 us (3%)
  local copies, waits for them, and re-layouts  9.85 us (2%)
  matrix products  8.79 us (1%)
    ppermute x8, waiting for transfers between devices, partner_2(): return lax.ppermute(value, axis, pairs)  484 us
    ppermute x8, starting transfers between devices, partner_2(): return lax.ppermute(value, axis, pairs)  20.5 us
    psum x1, waiting for transfers between devices, local(): lax.psum(filter_local, 'chan')  14.7 us
  transfers between devices with their start and end apart: 11, of which 10 were waited for; matrix products, arithmetic and copies ran while one was open for 2% of the time, Pallas kernels for 0%

commit v1 on v0

--- a/solution.py
+++ b/solution.py
@@ -1,8 +1,17 @@
+import functools
 import math
 import jax
 import jax.numpy as jnp
 from jax import lax
 from jax.sharding import PartitionSpec as P
+
+
+def shape_series(patch, axis_id):
+    y2 = lax.all_gather(patch, axis_id)
+    return jnp.sum(y2, axis=0)
+
+
+reach_the_panel = functools.partial(shape_series, axis_id="chan")
 
 
 def partner_2(value, axis, apart):
@@ -189,7 +198,7 @@
     conv_out = conv_part + skip_gain[:, None] * gated_prod
     gated_grad = corr_part + skip_gain[:, None] * gate_grad
     members_total = channels_dev * lax.axis_size("chan") // filters
-    filter_grad = lax.psum(filter_local, "chan") * (1.0 / math.sqrt(members_total * seq_total))
+    filter_grad = reach_the_panel(filter_local) * (1.0 / math.sqrt(members_total * seq_total))
     grads_in = jnp.stack([out_float * conv_out, gated_grad * values, gated_grad * gate_in])
     following = shifted(grads_in[:, :, :reach_back], "seq", -1)
     extended_grad = jnp.concatenate([grads_in, following], axis=2)

time: 612 us -> 583 us (0.953)
  waiting for transfers between devices: 503 us -> 486 us
  between operations: 15.8 us -> 2.41 us
    psum x1 -> x0, waiting for transfers between devices: 14.7 us -> none  [local(): lax.psum(filter_local, 'chan')]
  transfers between devices with their start and end apart: 11 -> 10, of which waited for: 10 -> 9; matrix products, arithmetic and copies ran while one was open for 2% -> 2% of each run, Pallas kernels for 0% -> 0%
where the time goes in v1:
time: 583 us; the launch traced here: 582 us
  waiting for transfers between devices  486 us (83%)
  other arithmetic  47.4 us (8%)
  starting transfers between devices  26.6 us (5%)
  matrix products  8.79 us (2%)
  local copies, waits for them, and re-layouts  8.57 us (1%)
    ppermute x8, waiting for transfers between devices, partner_2(): return lax.ppermute(value, axis, pairs)  484 us
    ppermute x8, starting transfers between devices, partner_2(): return lax.ppermute(value, axis, pairs)  20.5 us
  transfers between devices with their start and end apart: 10, of which 9 were waited for; matrix products, arithmetic and copies ran while one was open for 2% of the time, Pallas kernels for 0%

profile of v1, /device:TPU:0, one launch (start us, length us, event | category | flops | bytes accessed | tf_op | source)
XLA Modules:
  0.0 581.7 jit_solution(15868399910879631035)
XLA Ops:
  0.6 1.2 copy.19
  1.8 4.8 collective-permute-start
  6.7 1.0 fusion.52
  7.8 1.0 copy.18
  8.9 1.0 copy.21
  9.9 0.6 fusion.26
  10.9 1.9 select_maximum_fusion
  12.8 3.4 collective-permute-start.1
  16.4 100.9 %collective-permute-done.1 = f32[1152,512]{0,1:T(8,128)} collective-permute-done((f32[1152,512]{0,1:T(8,128)}, f32[1152,512]{0,1:T(8,128)}, u32[]{:S(2)}, u32[]{:S(2)}) %collective-permute-start.1) | collective-permute-done | bytes 2359328 | tf_op jit(solution)/shard_map/ppermute | solution.py:20
  117.3 2.1 fusion.50
  119.7 2.5 maximum_select_fusion
  122.2 0.7 collective-permute-start.2
  123.1 51.3 %collective-permute-done.2 = f32[1152,512]{0,1:T(8,128)} collective-permute-done((f32[1152,512]{0,1:T(8,128)S(1)}, f32[1152,512]{0,1:T(8,128)}, u32[]{:S(2)}, u32[]{:S(2)}) %collective-permute-start.2) | collective-permute-done | bytes 2359328 | tf_op jit(solution)/shard_map/ppermute | solution.py:20
  174.5 1.9 sub.100
  176.4 0.2 multiply_subtract_fusion.8
  176.6 3.5 maximum_select_fusion.1
  180.1 1.5 collective-permute-start.3
  181.9 50.0 %collective-permute-done.3 = f32[1152,512]{0,1:T(8,128)S(1)} collective-permute-done((f32[1152,512]{0,1:T(8,128)}, f32[1152,512]{0,1:T(8,128)S(1)}, u32[]{:S(2)}, u32[]{:S(2)}) %collective-permute-start.3) | collective-permute-done | bytes 2359328 | tf_op jit(solution)/shard_map/ppermute | solution.py:20
  231.8 2.8 sub.102
  234.6 0.2 multiply_subtract_fusion.7
  234.9 2.8 maximum_select_fusion.2
  237.7 1.6 collective-permute-start.4
  239.3 0.6 multiply_sine_fusion.1
  239.9 1.0 fusion.42
  240.9 1.7 fusion.43
  242.6 1.0 multiply_sine_fusion
  243.6 1.8 sine_multiply_fusion
  245.4 43.0 %collective-permute-done.4 = f32[1152,512]{0,1:T(8,128)} collective-permute-done((f32[1152,512]{0,1:T(8,128)S(1)}, f32[1152,512]{0,1:T(8,128)}, u32[]{:S(2)}, u32[]{:S(2)}) %collective-permute-start.4) | collective-permute-done | bytes 2359328 | tf_op jit(solution)/shard_map/ppermute | solution.py:20
  288.4 1.9 sub.104
  290.5 2.1 maximum_select_fusion.3
  292.6 0.3 multiply_subtract_fusion.5
  292.9 4.0 fusion
  297.0 0.9 multiply_subtract_fusion.10
  297.9 1.0 multiply_subtract_fusion.11
  299.1 0.7 reduce_sum.28
  299.8 1.1 pad_maximum_fusion.8
  300.8 0.7 reduce_sum.27
  301.9 0.5 copy-done.16
  303.2 4.8 fusion.11
  308.0 0.3 multiply_subtract_fusion.4
  308.5 1.6 collective-permute-start.5
  310.0 48.1 %collective-permute-done.5 = f32[1152,512]{0,1:T(8,128)S(1)} collective-permute-done((f32[1152,512]{0,1:T(8,128)S(1)}, f32[1152,512]{0,1:T(8,128)S(1)}, u32[]{:S(2)}, u32[]{:S(2)}) %collective-permute-start.5) | collective-permute-done | bytes 2359328 | tf_op jit(solution)/shard_map/ppermute | solution.py:20
  358.6 0.6 select_multiply_fusion.3
  359.2 1.6 collective-permute-start.6
  361.0 47.1 %collective-permute-done.6 = f32[1152,512]{0,1:T(8,128)} collective-permute-done((f32[1152,512]{0,1:T(8,128)S(1)}, f32[1152,512]{0,1:T(8,128)}, u32[]{:S(2)}, u32[]{:S(2)}) %collective-permute-start.6) | collective-permute-done | bytes 2359328 | tf_op jit(solution)/shard_map/ppermute | solution.py:20
  408.1 1.9 broadcast_select_fusion.1
  410.0 0.2 multiply_subtract_fusion.2
  410.3 1.8 select_multiply_fusion.2
  412.1 5.1 collective-permute-start.7
  417.4 46.9 %collective-permute-done.7 = f32[1152,512]{0,1:T(8,128)S(1)} collective-permute-done((f32[1152,512]{0,1:T(8,128)}, f32[1152,512]{0,1:T(8,128)S(1)}, u32[]{:S(2)}, u32[]{:S(2)}) %collective-permute-start.7) | collective-permute-done | bytes 2359328 | tf_op jit(solution)/shard_map/ppermute | solution.py:20
  464.6 1.2 copy-done.3
  466.0 2.1 select_multiply_fusion.1
  468.1 5.0 collective-permute-start.8
  473.3 96.8 %collective-permute-done.8 = f32[1152,512]{0,1:T(8,128)} collective-permute-done((f32[1152,512]{0,1:T(8,128)S(1)}, f32[1152,512]{0,1:T(8,128)}, u32[]{:S(2)}, u32[]{:S(2)}) %collective-permute-start.8) | collective-permute-done | bytes 2359328 | tf_op jit(solution)/shard_map/ppermute | solution.py:20
  570.1 1.9 broadcast_select_fusion.3
  572.3 0.4 select_multiply_fusion
  573.0 0.5 fusion.33
  573.5 0.6 copy-done.5
  574.3 1.3 collective-permute-start.9
  575.7 1.9 all-gather
  577.6 0.6 broadcast_multiply_fusion.2
  578.3 1.8 collective-permute-done.9
  580.1 0.7 fusion.20
  580.8 0.9 copy.23
  (94 shorter events, 3.8 us)
Async XLA Ops:
  1.8 8.0 %collective-permute-start = (bf16[3,256,6]{1,2,0:T(8,128)(2,1)S(1)}, bf16[3,256,6]{1,2,0:T(8,128)(2,1)S(1)}, u32[]{:S(2)}, u32[]{:S(2)}) collective-permute-start(bf16[3,256,6]{1,2,0:T(8,128)(2,1)S(1)} %slice.304), channel_id=1, source_target_pairs={{0,2},{2,4},{4,6},{6,8},{8,10},{10,12},{12,14},{14,16},{16,18},{18... | collective-permute-start | bytes 27656 | tf_op jit(solution)/shard_map/ppermute | solution.py:26
  7.7 2.9 copy-start.17
  7.7 2.9 copy-start.19
  7.8 2.9 copy-start.23
  7.8 2.9 copy-start.25
  7.8 2.8 copy-start.21
  8.8 1.8 copy-start.6
  10.6 2.2 copy-start.4
  10.9 108.5 %copy-start = (f32[576,256]{0,1:T(8,128)}, f32[576,256]{0,1:T(8,128)S(1)}, u32[]{:S(2)}) copy-start(f32[576,256]{0,1:T(8,128)S(1)} %get-tuple-element.48) | copy-start | bytes 1769476
  10.9 108.5 %copy-start.1 = (f32[576,256]{0,1:T(8,128)}, f32[576,256]{0,1:T(8,128)S(1)}, u32[]{:S(2)}) copy-start(f32[576,256]{0,1:T(8,128)S(1)} %get-tuple-element.49) | copy-start | bytes 1769476
  12.8 104.5 %collective-permute-start.1 = (f32[1152,512]{0,1:T(8,128)}, f32[1152,512]{0,1:T(8,128)}, u32[]{:S(2)}, u32[]{:S(2)}) collective-permute-start(f32[1152,512]{0,1:T(8,128)} %select_maximum_fusion), channel_id=1, source_target_pairs={{0,16},{2,18},{4,20},{6,22},{8,24},{10,26},{12,28},{14,30},{16,0},... | collective-permute-start | bytes 7077896 | tf_op jit(solution)/shard_map/ppermute | solution.py:20
  122.2 52.3 %collective-permute-start.2 = (f32[1152,512]{0,1:T(8,128)S(1)}, f32[1152,512]{0,1:T(8,128)}, u32[]{:S(2)}, u32[]{:S(2)}) collective-permute-start(f32[1152,512]{0,1:T(8,128)S(1)} %maximum_select_fusion), channel_id=1, source_target_pairs={{0,8},{2,10},{4,12},{6,14},{8,0},{10,2},{12,4},{14,6},{16,24},{18,... | collective-permute-start | bytes 7077896 | tf_op jit(solution)/shard_map/ppermute | solution.py:20
  180.1 51.7 %collective-permute-start.3 = (f32[1152,512]{0,1:T(8,128)}, f32[1152,512]{0,1:T(8,128)S(1)}, u32[]{:S(2)}, u32[]{:S(2)}) collective-permute-start(f32[1152,512]{0,1:T(8,128)} %maximum_select_fusion.1), channel_id=1, source_target_pairs={{0,4},{2,6},{4,0},{6,2},{8,12},{10,14},{12,8},{14,10},{16,20},{18,... | collective-permute-start | bytes 7077896 | tf_op jit(solution)/shard_map/ppermute | solution.py:20
  231.8 2.8 copy-start.2
  237.7 50.7 %collective-permute-start.4 = (f32[1152,512]{0,1:T(8,128)S(1)}, f32[1152,512]{0,1:T(8,128)}, u32[]{:S(2)}, u32[]{:S(2)}) collective-permute-start(f32[1152,512]{0,1:T(8,128)S(1)} %maximum_select_fusion.2), channel_id=1, source_target_pairs={{0,2},{2,0},{4,6},{6,4},{8,10},{10,8},{12,14},{14,12},{16,18},{18,... | collective-permute-start | bytes 7077896 | tf_op jit(solution)/shard_map/ppermute | solution.py:20
  301.6 0.9 copy-start.16
  301.6 1.0 copy-start.10
  301.6 1.1 copy-start.11
  301.7 1.0 copy-start.8
  301.8 1.1 copy-start.9
  301.8 1.2 copy-start.15
  301.8 1.2 copy-start.12
  301.8 1.3 copy-start.13
  301.8 1.4 copy-start.14
  303.2 4.8 copy-start.27
  303.2 4.8 copy-start.28
  308.5 49.7 %collective-permute-start.5 = (f32[1152,512]{0,1:T(8,128)S(1)}, f32[1152,512]{0,1:T(8,128)S(1)}, u32[]{:S(2)}, u32[]{:S(2)}) collective-permute-start(f32[1152,512]{0,1:T(8,128)S(1)} %pad_maximum_fusion), channel_id=1, source_target_pairs={{0,2},{2,0},{4,6},{6,4},{8,10},{10,8},{12,14},{14,12},{16,18},{18,... | collective-permute-start | bytes 7077896 | tf_op jit(solution)/shard_map/ppermute | solution.py:20
  359.2 48.9 %collective-permute-start.6 = (f32[1152,512]{0,1:T(8,128)S(1)}, f32[1152,512]{0,1:T(8,128)}, u32[]{:S(2)}, u32[]{:S(2)}) collective-permute-start(f32[1152,512]{0,1:T(8,128)S(1)} %select_multiply_fusion.3), channel_id=1, source_target_pairs={{0,4},{2,6},{4,0},{6,2},{8,12},{10,14},{12,8},{14,10},{16,20},{18,... | collective-permute-start | bytes 7077896 | tf_op jit(solution)/shard_map/ppermute | solution.py:20
  412.1 52.2 %collective-permute-start.7 = (f32[1152,512]{0,1:T(8,128)}, f32[1152,512]{0,1:T(8,128)S(1)}, u32[]{:S(2)}, u32[]{:S(2)}) collective-permute-start(f32[1152,512]{0,1:T(8,128)} %select_multiply_fusion.2), channel_id=1, source_target_pairs={{0,8},{2,10},{4,12},{6,14},{8,0},{10,2},{12,4},{14,6},{16,24},{18,... | collective-permute-start | bytes 7077896 | tf_op jit(solution)/shard_map/ppermute | solution.py:20
  464.3 1.5 copy-start.3
  468.1 102.0 %collective-permute-start.8 = (f32[1152,512]{0,1:T(8,128)S(1)}, f32[1152,512]{0,1:T(8,128)}, u32[]{:S(2)}, u32[]{:S(2)}) collective-permute-start(f32[1152,512]{0,1:T(8,128)S(1)} %select_multiply_fusion.1), channel_id=1, source_target_pairs={{0,16},{2,18},{4,20},{6,22},{8,24},{10,26},{12,28},{14,30},{16,0},... | collective-permute-start | bytes 7077896 | tf_op jit(solution)/shard_map/ppermute | solution.py:20
  572.3 0.6 copy-start.24
  572.3 0.7 copy-start.26
  573.0 1.1 copy-start.5
  573.0 1.1 copy-start.7
  573.0 1.1 copy-start.29
  574.2 5.9 %copy-start.18 = (f32[3,256]{1,0:T(4,128)S(1)}, f32[3,256]{1,0:T(4,128)}, u32[]{:S(2)}) copy-start(f32[3,256]{1,0:T(4,128)} %copy-done.17) | copy-start | bytes 9220
  574.2 5.9 %copy-start.20 = (f32[3,256]{1,0:T(4,128)S(1)}, f32[3,256]{1,0:T(4,128)}, u32[]{:S(2)}) copy-start(f32[3,256]{1,0:T(4,128)} %copy-done.19) | copy-start | bytes 9220
  574.2 5.9 %copy-start.22 = (f32[3,1,256]{2,0,1:T(4,128)S(1)}, f32[3,1,256]{2,0,1:T(4,128)}, u32[]{:S(2)}) copy-start(f32[3,1,256]{2,0,1:T(4,128)} %copy-done.21) | copy-start | bytes 9220
  574.3 5.7 collective-permute-start.9
